TPU v7x, 768 devices: a whole 4x8x12 slice. The times are simulated.
768 devices in a mesh: img: 96 (over x, y, z_lo), txt: 8 (over z_hi, core).
Axes of the slice: x: 4, y: 8, z: 12 (z_hi: 4, z_lo: 3; z = z_hi * 3 + z_lo), core: 2. Of those that a mesh axis runs over, the one named last changes fastest.
Arguments:
- image_emb: float32 [12288, 768], P(('img', 'txt')), may hold values from -0.6 to 0.6
- text_emb: float32 [12288, 768], P(('txt', 'img')), may hold values from -0.6 to 0.6
- pairs: int32 [12288], P('img'), may hold values from 0 to 12287, each once
- log_scale: float32 [1], replicated, may hold values from 2 to 2.6
- bias: float32 [1], replicated, may hold values from -12 to -8
Outputs:
- image_loss: float32 [12288], P('img')
- image_grad: float32 [12288, 768], P(('img', 'txt'))
- text_grad: float32 [12288, 768], P(('txt', 'img'))
Inputs may be any that keep to these rules, and one draw needn't show every extreme that they name: `pairs`: each text is matched to exactly one image.
All inputs are finite; a program needn't handle non-finite values.
Results may differ from a plain program's by a relative error of at most 0.0003.
Values sent between devices are 32-bit elements; how exact they have to be, the bound alone decides.
A program may use at most 32 MiB of HBM per device.

v0:
```python
import jax
import jax.numpy as jnp
from jax import lax
from jax.sharding import PartitionSpec as P


def per_device(image_emb, text_emb, pairs, log_scale, bias):
    images = lax.all_gather(image_emb, "txt", axis=0, tiled=True)
    texts = lax.all_gather(text_emb, "img", axis=0, tiled=True)
    scale = jnp.exp(log_scale[0])
    shift = bias[0]
    text_count = texts.shape[0]
    dots = lax.dot_general(
        images,
        texts,
        (((1,), (1,)), ((), ())),
        precision=lax.Precision.HIGHEST,
        preferred_element_type=jnp.float32,
    )
    logits = scale * dots + shift
    columns = lax.axis_index("txt") * text_count + jnp.arange(text_count, dtype=jnp.int32)
    sign = jnp.where(pairs[:, None] == columns[None, :], 1.0, -1.0).astype(jnp.float32)
    loss_part = jnp.sum(jax.nn.softplus(-sign * logits), axis=1)
    image_loss = lax.psum(loss_part, "txt")
    dlogits = -sign * jax.nn.sigmoid(-sign * logits)
    image_term = scale * jnp.dot(
        dlogits, texts, precision=lax.Precision.HIGHEST, preferred_element_type=jnp.float32
    )
    image_grad = lax.psum_scatter(image_term, "txt", scatter_dimension=0, tiled=True)
    text_term = scale * lax.dot_general(
        dlogits,
        images,
        (((0,), (0,)), ((), ())),
        precision=lax.Precision.HIGHEST,
        preferred_element_type=jnp.float32,
    )
    text_grad = lax.psum_scatter(text_term, "img", scatter_dimension=0, tiled=True)
    return (image_loss, image_grad, text_grad)


def solution(mesh):
    return jax.shard_map(
        per_device,
        mesh=mesh,
        in_specs=(P(("img", "txt"), None), P(("txt", "img"), None), P("img"), P(), P()),
        out_specs=(P("img"), P(("img", "txt"), None), P(("txt", "img"), None)),
        check_vma=False,
    )
```

profile of v0, /device:TPU:192, one launch (start us, length us, event | category | flops | bytes accessed | tf_op | source)
XLA Modules:
  0.0 1208.9 jit_solution(9175986057524945769)
XLA Ops:
  7.2 0.0 copy-start.1
  7.2 0.0 all-gather.2.cloned.1.call-start
  7.2 0.7 all-gather.2.cloned.1.call-update
  7.9 0.0 reduce-scatter.3.cloned.1.call-start
  9.3 23.5 %all_gather.6 = f32[128,768]{1,0:T(8,128)S(1)} all-gather(f32[16,768]{1,0:T(8,128)} %param.5), channel_id=1, replica_groups=mesh['img'=96,'txt'=8] {'txt'}, dimensions={0}, use_global_device_ids=true | all-gather | bytes 442368 | tf_op jit(solution)/shard_map/all_gather | solution.py:8
  32.8 534.9 %all-gather.2.cloned.1.call-done = f32[1536,768]{1,0:T(8,128)} async-done(((f32[16,768]{1,0:T(8,128)}), f32[1536,768]{1,0:T(8,128)}) %all-gather.2.cloned.1.call-update) | async-done | bytes 4718608 | tf_op jit(solution)/shard_map/all_gather | solution.py:9
  567.7 0.0 copy-start
  567.7 7.6 fusion.2
  575.3 0.0 copy-done.1
  575.3 0.0 copy-done
  575.3 3.6 convolution_multiply_fusion.2
  579.0 0.0 reduce-scatter.3.cloned.1.call-update
  579.0 0.0 reduce-scatter.5.cloned.1.call-start
  579.0 5.8 convolution_multiply_fusion
  584.8 0.0 reduce-scatter.5.cloned.1.call-update
  584.8 14.5 %psum.7 = f32[128]{0:T(128)} all-reduce(f32[128]{0:T(128)S(1)} %get-tuple-element.3), channel_id=1, replica_groups=mesh['img'=96,'txt'=8] {'txt'}, use_global_device_ids=true, to_apply=%region_1.2 | all-reduce | flops 128 | bytes 1024 | tf_op jit(solution)/shard_map/psum | solution.py:24
  599.4 12.6 %reduce-scatter.3.cloned.1.call-done = f32[16,768]{1,0:T(8,128)} async-done(((f32[128,768]{1,0:T(8,128)}), f32[16,768]{1,0:T(8,128)}) %reduce-scatter.3.cloned.1.call-update) | async-done | bytes 49168 | tf_op jit(solution)/shard_map/reduce_scatter | solution.py:29
  612.0 590.4 %reduce-scatter.5.cloned.1.call-done = f32[16,768]{1,0:T(8,128)} async-done(((f32[1536,768]{1,0:T(8,128)}), f32[16,768]{1,0:T(8,128)}) %reduce-scatter.5.cloned.1.call-update) | async-done | bytes 49168 | tf_op jit(solution)/shard_map/reduce_scatter | solution.py:37
  (1 shorter events, 0.0 us)
Async XLA Ops:
  7.2 568.1 %copy-start.1 = (s32[128]{0:T(128)S(1)}, s32[128]{0:T(128)}, u32[]{:S(2)}) copy-start(s32[128]{0:T(128)} %param.7) | copy-start | bytes 1540
  7.2 560.5 %all-gather.2.cloned.1.call-start = ((), (), s32[]{:S(2)}) async-start(), calls=%async_computation.2 | async-start | bytes 4767744 | tf_op jit(solution)/shard_map/all_gather | solution.py:9
  7.9 604.1 %reduce-scatter.3.cloned.1.call-start = ((), (), s32[]{:S(2)}) async-start(), calls=%async_computation.3 | async-start | bytes 442368 | tf_op jit(solution)/shard_map/reduce_scatter | solution.py:29
  567.7 7.6 copy-start
  579.0 623.4 %reduce-scatter.5.cloned.1.call-start = ((), (), s32[]{:S(2)}) async-start(), calls=%async_computation.4 | async-start | bytes 4767744 | tf_op jit(solution)/shard_map/reduce_scatter | solution.py:37
Sparse Core Ops, SparseCore 0:
  10.4 557.2 all-gather.1
  579.1 32.8 reduce-scatter.2
  616.0 586.3 reduce-scatter.4
where the time goes:
time: 1210 us
  waiting for transfers between devices  1140 us (94%)
  blocking collectives  38 us (3%)
  matrix products  17.1 us (1%)
  between operations  15.1 us (1%)
    reduce_scatter x1, waiting for transfers between devices, per_device(): lax.psum_scatter(text_term, 'img', scatter_dimension=0, tiled=True)  590 us
    all_gather x1, waiting for transfers between devices, per_device(): texts = lax.all_gather(text_emb, 'img', axis=0, tiled=True)  535 us
  transfers between devices with their start and end apart: 3, of which 3 were waited for; matrix products, arithmetic and copies ran while one was open for 0% of the time, Pallas kernels for 0%

commit v1 on v0

v1 whole, which is shorter than its diff:
```python
import functools

import jax
import jax.numpy as jnp
from jax import lax
from jax.experimental import pallas as pl
from jax.experimental.pallas import tpu as pltpu
from jax.sharding import PartitionSpec as P

MESH = pl.DeviceIdType.MESH
NX, NY, NZ, ZLO = 4, 8, 12, 3
ROWS, WIDTH = 16, 768
CA = 256
CB = WIDTH - CA
TEXTS = 2 * NZ * ROWS
F32, BF16 = jnp.float32, jnp.bfloat16
COPIES = 128
STEP = (0, 1, -1)


def halves(value):
    high = value.astype(BF16)
    return high, (value - high.astype(F32)).astype(BF16)


def dot3(ah, al, bh, bl, dims):
    def dot(a, b):
        return lax.dot_general(a, b, (dims, ((), ())), preferred_element_type=F32)

    return dot(ah, bh) + (dot(ah, bl) + dot(al, bh))


def kernel(
    log_scale_ref, bias_ref, pairs_ref, image_ref, text_ref,
    loss_ref, image_grad_ref, text_grad_ref,
    ga, gb, tx, xh, xl, th, tl, dh, dl, pc,
    xga, xgb, tg, rxb, rya, ryb, rxa, rc, rz, rk, py, px, ly, lx, lz,
    local_sem, send_sem, recv_sem,
):
    img, txt = lax.axis_index("img"), lax.axis_index("txt")
    column = lax.div(img, ZLO)
    x, y = lax.div(column, NY), lax.rem(column, NY)
    core = lax.rem(txt, 2)
    z = lax.div(txt, 2) * ZLO + lax.rem(img, ZLO)
    way = 1 - 2 * core

    def moved(at, by, size):
        return lax.rem(at + way * by + 2 * size, size)

    def device(at_x, at_y, at_z, at_core):
        return (
            (at_x * NY + at_y) * ZLO + lax.rem(at_z, ZLO),
            lax.div(at_z, ZLO) * 2 + at_core,
        )

    def along_x(by):
        return device(moved(x, by, NX), y, z, core)

    def along_y(by):
        return device(x, moved(y, by, NY), z, core)

    def along_z(by):
        return device(x, y, moved(z, by, NZ), core)

    sibling = device(x, y, z, 1 - core)
    peers = [along_x(by) for by in (1, -1, 2)]
    peers += [along_y(by) for by in (1, -1, 2, -2)]
    peers += [along_z(by) for by in (1, -1, 3, -3, 6)]
    peers.append(sibling)

    copies = [
        pltpu.make_async_copy(image_ref.at[:, pl.ds(0, CA)], ga.at[0, 0], local_sem.at[0]),
        pltpu.make_async_copy(image_ref.at[:, pl.ds(CA, CB)], gb.at[0, 0], local_sem.at[1]),
        pltpu.make_async_copy(text_ref, tx.at[0, 0, 0], local_sem.at[2]),
    ]
    for copy in copies:
        copy.start()

    barrier = pltpu.get_barrier_semaphore()
    for peer in peers:
        pl.semaphore_signal(barrier, inc=1, device_id=peer, device_id_type=MESH)

    lane = lax.broadcasted_iota(jnp.int32, (8, 128), 1)
    row = lax.broadcasted_iota(jnp.int32, (8, 128), 0)
    own = 2 * (x * NY + y)
    pairs_row = jnp.broadcast_to(pairs_ref[...].astype(F32), (8, 128))
    tile = jnp.zeros((8, 128), F32)
    for half in range(2):
        picked = jnp.where(lane == txt * ROWS + half * 8 + row, pairs_row, 0.0)
        tile = jnp.where(lane == own + half, jnp.sum(picked, axis=1, keepdims=True), tile)
    py[0] = tile

    pl.semaphore_wait(barrier, len(peers))
    for copy in copies:
        copy.wait()

    started = []

    def send(source, target, to):
        at = len(started)
        copy = pltpu.make_async_remote_copy(
            src_ref=source,
            dst_ref=target,
            send_sem=send_sem.at[at],
            recv_sem=recv_sem.at[at],
            device_id=to,
            device_id_type=MESH,
        )
        copy.start()
        started.append(copy)
        return copy

    def arrived(*copies):
        for copy in copies:
            copy.wait_recv()

    a_x = [send(ga.at[0, 0], ga.at[0, by % NX], along_x(by)) for by in (2, 1, -1)]
    b_y2 = [send(gb.at[0, 0], gb.at[0, by % NY], along_y(by)) for by in (2, -2)]
    t6 = send(tx.at[0, 0, 0], tx.at[0, 0, 2], along_z(6))
    t3 = [send(tx.at[0, 0, 0], tx.at[0, 0, k], along_z(by)) for k, by in ((1, 3), (3, -3))]
    b_y1 = [send(gb.at[0, 0], gb.at[0, by % NY], along_y(by)) for by in (1, -1)]
    p_y2 = [send(py.at[0], py.at[by % NY], along_y(by)) for by in (2, -2)]
    p_y1 = [send(py.at[0], py.at[by % NY], along_y(by)) for by in (1, -1)]
    t_near = [send(tx.at[0, 0, 0], tx.at[0, e, 0], along_z(STEP[e])) for e in (1, 2)]
    b_x = [send(gb.at[0, 0], gb.at[by % NX, 0], along_x(by)) for by in (2, 1, -1)]

    arrived(*a_x)
    a_y2 = [send(ga.at[0], ga.at[by % NY], along_y(by)) for by in (2, -2)]
    arrived(*b_y2)
    b_far = [
        send(gb.at[0, 2], gb.at[0, 4], along_y(2)),
        send(gb.at[0, 2], gb.at[0, 3], along_y(1)),
        send(gb.at[0, 6], gb.at[0, 5], along_y(-1)),
    ]
    a_y1 = [send(ga.at[0], ga.at[by % NY], along_y(by)) for by in (1, -1)]
    arrived(*b_y1)
    for low in (1, 6):
        b_x += [
            send(gb.at[0, pl.ds(low, 2)], gb.at[by % NX, pl.ds(low, 2)], along_x(by))
            for by in (2, 1, -1)
        ]
    arrived(*p_y2)
    p_far = [
        send(py.at[2], py.at[4], along_y(2)),
        send(py.at[2], py.at[3], along_y(1)),
        send(py.at[6], py.at[5], along_y(-1)),
    ]
    arrived(*t3)
    for k in (1, 3):
        t_near += [send(tx.at[0, 0, k], tx.at[0, e, k], along_z(STEP[e])) for e in (1, 2)]
    arrived(*a_y2)
    a_far = [
        send(ga.at[2], ga.at[4], along_y(2)),
        send(ga.at[2], ga.at[3], along_y(1)),
        send(ga.at[6], ga.at[5], along_y(-1)),
    ]
    arrived(*b_far)
    b_x += [
        send(gb.at[0, pl.ds(3, 3)], gb.at[by % NX, pl.ds(3, 3)], along_x(by))
        for by in (2, 1, -1)
    ]
    arrived(t6)
    t_near += [send(tx.at[0, 0, 2], tx.at[0, e, 2], along_z(STEP[e])) for e in (1, 2)]
    t_core = [send(tx.at[0, 0], tx.at[1, 0], sibling)]
    arrived(*p_y1, *p_far)
    px[0] = jnp.sum(py[...], axis=0)
    p_x = [send(px.at[0], px.at[by % NX], along_x(by)) for by in (2, 1, -1)]

    places = lax.broadcasted_iota(jnp.int32, (8, TEXTS), 1)
    slot = lax.div(places, ROWS)
    ids = places
    for s in range(2):
        for e in range(3):
            for k in range(4):
                at = (s * 3 + e) * 4 + k
                by = 3 * k + STEP[e]
                at_z = moved(z, by if s else -by, NZ)
                at_core = 1 - core if s else core
                owner = lax.div(at_z, ZLO) * 2 + at_core
                base = owner * (NX * NY * ZLO * ROWS) + (column * ZLO + lax.rem(at_z, ZLO)) * ROWS
                ids = jnp.where(slot == at, places + (base - at * ROWS), ids)
    ids = ids.astype(F32)[0:1]

    arrived(*t_near)
    t_core.append(send(tx.at[0, pl.ds(1, 2)], tx.at[1, pl.ds(1, 2)], sibling))

    arrived(*p_x)
    matched = jnp.sum(px[...], axis=0)

    def lane_of(ox, oy, half):
        return 2 * (moved(x, -ox, NX) * NY + moved(y, -oy, NY)) + half

    for ox in range(NX):
        for oy in range(NY):
            for half in range(2):
                picked = jnp.where(lane == lane_of(ox, oy, half), matched, 0.0)
                spread = jnp.broadcast_to(jnp.sum(picked, axis=1, keepdims=True), (8, 128))
                pc[pl.ds(((ox * NY + oy) * 2 + half) * 8, 8), :] = spread

    arrived(*t_core)
    for s in range(2):
        high, low = halves(tx[s].reshape(NZ * ROWS, WIDTH))
        th[pl.ds(s * NZ * ROWS, NZ * ROWS), :] = high
        tl[pl.ds(s * NZ * ROWS, NZ * ROWS), :] = low
    arrived(*a_y1, *a_far)
    for ox in range(NX):
        high, low = halves(ga[:, ox].reshape(NY * ROWS, CA))
        xh[pl.ds(ox * NY * ROWS, NY * ROWS), pl.ds(0, CA)] = high
        xl[pl.ds(ox * NY * ROWS, NY * ROWS), pl.ds(0, CA)] = low
    arrived(*b_x)
    for ox in range(NX):
        high, low = halves(gb[ox].reshape(NY * ROWS, CB))
        xh[pl.ds(ox * NY * ROWS, NY * ROWS), pl.ds(CA, CB)] = high
        xl[pl.ds(ox * NY * ROWS, NY * ROWS), pl.ds(CA, CB)] = low

    scale = jnp.exp(jnp.full((8, 128), log_scale_ref[0], F32))[0:1, 0:1]
    shift = bias_ref[0]
    losses = jnp.zeros((8, 128), F32)
    r_x = []
    for ox in (2, 1, 3, 0):
        rows = pl.ds(ox * NY * ROWS, NY * ROWS)
        dots = dot3(xh[rows, :], xl[rows, :], th[...], tl[...], ((1,), (1,)))
        logits = scale * dots + shift
        pair = pc[rows, :]
        match = jnp.concatenate([pair] * (TEXTS // 128), axis=1) == ids
        signed = jnp.where(match, -logits, logits)
        small = jnp.exp(-jnp.abs(logits))
        loss = jnp.maximum(signed, 0.0) + jnp.log1p(small)
        loss = sum(loss[:, at * 128 : (at + 1) * 128] for at in range(TEXTS // 128))
        loss = jnp.sum(loss, axis=1, keepdims=True)
        for oy in range(NY):
            for half in range(2):
                at = (oy * 2 + half) * 8
                losses = jnp.where(lane == lane_of(ox, oy, half), loss[at : at + 8], losses)
        part = 1.0 / (1.0 + small)
        chance = jnp.where(signed >= 0.0, part, small * part)
        slope = scale * jnp.where(match, -chance, chance)
        high, low = halves(slope)
        dh[rows, :] = high
        dl[rows, :] = low
        grad = dot3(high, low, th[...], tl[...], ((1,), (0,)))
        xgb[ox] = grad[:, CA:].reshape(NY, ROWS, CB)
        for oy in range(NY):
            xga[oy, ox] = grad[oy * ROWS : (oy + 1) * ROWS, :CA]
        if ox:
            r_x.append(send(xgb.at[ox], rxb.at[ox - 1], along_x(-ox)))
    ly[0] = losses
    l_y2 = [send(ly.at[0], ly.at[by % NY], along_y(by)) for by in (2, -2)]
    l_y1 = [send(ly.at[0], ly.at[by % NY], along_y(by)) for by in (1, -1)]

    def y_first(source, target):
        far = [
            send(source(4), target(4), along_y(-2)),
            send(source(3), target(3), along_y(-1)),
            send(source(5), target(5), along_y(1)),
        ]
        near = [send(source(1), target(1), along_y(-1)), send(source(7), target(7), along_y(1))]
        return far, near

    def y_second(source, target, far):
        arrived(*far)
        source(2)[...] += target(3)[...] + target(4)[...]
        source(6)[...] += target(5)[...]
        return [send(source(2), target(2), along_y(-2)), send(source(6), target(6), along_y(2))]

    a_far, a_near = y_first(lambda o: xga.at[o], lambda o: rya.at[o])

    def text_part(at):
        cols = pl.ds(at * 128, 128)
        part = dot3(dh[:, cols], dl[:, cols], xh[...], xl[...], ((0,), (0,)))
        part = part.reshape(8, ROWS, WIDTH)
        for i in range(8):
            s, rest = divmod(at * 8 + i, 12)
            e, k = divmod(rest, 4)
            tg[s, e, k] = part[i]

    text_part(2)
    text_part(1)
    r_core = send(tg.at[1], rc, sibling)
    arrived(*l_y2)
    l_far = [
        send(ly.at[2], ly.at[4], along_y(2)),
        send(ly.at[2], ly.at[3], along_y(1)),
        send(ly.at[6], ly.at[5], along_y(-1)),
    ]
    text_part(0)
    arrived(r_core)
    for e in (1, 2, 0):
        tg[0, e] += rc[e]
        if e:
            rz_copy = send(tg.at[0, e], rz.at[e - 1], along_z(-STEP[e]))
            r_z = [rz_copy] if e == 1 else r_z + [rz_copy]

    a_late = y_second(lambda o: xga.at[o], lambda o: rya.at[o], a_far)
    arrived(*l_y1, *l_far)
    lx[0] = jnp.sum(ly[...], axis=0)
    l_x = [send(lx.at[0], lx.at[by % NX], along_x(by)) for by in (2, 1, -1)]

    arrived(*r_z)
    tg[0, 0] += rz[0] + rz[1]
    r_k = [send(tg.at[0, 0, k], rk.at[k - 1], along_z(-3 * k)) for k in (2, 1, 3)]

    arrived(*l_x)
    lz[0, 0] = jnp.sum(lx[...], axis=0)
    l_core = send(lz.at[0, 0], lz.at[0, 1], sibling)

    arrived(*r_x)
    xgb[0] += rxb[0] + rxb[1] + rxb[2]
    b_far, b_near = y_first(lambda o: xgb.at[0, o], lambda o: ryb.at[o])

    arrived(l_core)
    l_z = [send(lz.at[0], lz.at[k], along_z(3 * k)) for k in (2, 1, 3)]

    arrived(*a_late, *a_near)
    xga[0] += (rya[1] + rya[7]) + (rya[2] + rya[6])
    r_a = [send(xga.at[0, ox], rxa.at[ox - 1], along_x(-ox)) for ox in (2, 1, 3)]

    b_late = y_second(lambda o: xgb.at[0, o], lambda o: ryb.at[o], b_far)

    arrived(*r_a)
    image_grad_ref[:, pl.ds(0, CA)] = xga[0, 0] + rxa[0] + rxa[1] + rxa[2]
    arrived(*r_k)
    text_grad_ref[...] = tg[0, 0, 0] + rk[0] + rk[1] + rk[2]

    arrived(*b_near, *b_late)
    image_grad_ref[:, pl.ds(CA, CB)] = xgb[0, 0] + (ryb[1] + ryb[7]) + (ryb[2] + ryb[6])

    arrived(*l_z)
    out = jnp.zeros((8, 128), F32)
    for k in range(4):
        for s in range(2):
            at_txt = lax.div(moved(z, -3 * k, NZ), ZLO) * 2 + (1 - core if s else core)
            for half in range(2):
                picked = jnp.where(lane == own + half, lz[k, s], 0.0)
                value = jnp.sum(picked, axis=1, keepdims=True)
                out = jnp.where(lane == at_txt * ROWS + half * 8 + row, value, out)
    loss_ref[...] = jnp.sum(out, axis=0, keepdims=True)

    for copy in started:
        copy.wait_send()


def per_device(image_emb, text_emb, pairs, log_scale, bias):
    vmem = pl.BlockSpec(memory_space=pltpu.VMEM)
    smem = pl.BlockSpec(memory_space=pltpu.SMEM)
    hbm = pl.BlockSpec(memory_space=pl.ANY)
    images = NX * NY * ROWS
    loss, image_grad, text_grad = pl.pallas_call(
        kernel,
        out_shape=(
            jax.ShapeDtypeStruct((1, 128), F32),
            jax.ShapeDtypeStruct((ROWS, WIDTH), F32),
            jax.ShapeDtypeStruct((ROWS, WIDTH), F32),
        ),
        in_specs=[smem, smem, vmem, hbm, hbm],
        out_specs=(vmem, vmem, vmem),
        scratch_shapes=[
            pltpu.VMEM((NY, NX, ROWS, CA), F32),
            pltpu.VMEM((NX, NY, ROWS, CB), F32),
            pltpu.VMEM((2, 3, 4, ROWS, WIDTH), F32),
            pltpu.VMEM((images, WIDTH), BF16),
            pltpu.VMEM((images, WIDTH), BF16),
            pltpu.VMEM((TEXTS, WIDTH), BF16),
            pltpu.VMEM((TEXTS, WIDTH), BF16),
            pltpu.VMEM((images, TEXTS), BF16),
            pltpu.VMEM((images, TEXTS), BF16),
            pltpu.VMEM((images, 128), F32),
            pltpu.VMEM((NY, NX, ROWS, CA), F32),
            pltpu.VMEM((NX, NY, ROWS, CB), F32),
            pltpu.VMEM((2, 3, 4, ROWS, WIDTH), F32),
            pltpu.VMEM((3, NY, ROWS, CB), F32),
            pltpu.VMEM((NY, NX, ROWS, CA), F32),
            pltpu.VMEM((NY, ROWS, CB), F32),
            pltpu.VMEM((3, ROWS, CA), F32),
            pltpu.VMEM((3, 4, ROWS, WIDTH), F32),
            pltpu.VMEM((2, 4, ROWS, WIDTH), F32),
            pltpu.VMEM((3, ROWS, WIDTH), F32),
            pltpu.VMEM((NY, 8, 128), F32),
            pltpu.VMEM((NX, 8, 128), F32),
            pltpu.VMEM((NY, 8, 128), F32),
            pltpu.VMEM((NX, 8, 128), F32),
            pltpu.VMEM((4, 2, 8, 128), F32),
            pltpu.SemaphoreType.DMA((3,)),
            pltpu.SemaphoreType.DMA((COPIES,)),
            pltpu.SemaphoreType.DMA((COPIES,)),
        ],
        compiler_params=pltpu.CompilerParams(
            collective_id=0, has_side_effects=True, vmem_limit_bytes=40 * 2**20
        ),
        name="contrastive",
    )(log_scale, bias, pairs.reshape(1, 128), image_emb, text_emb)
    return loss.reshape(128), image_grad, text_grad


def solution(mesh):
    return jax.shard_map(
        per_device,
        mesh=mesh,
        in_specs=(P(("img", "txt"), None), P(("txt", "img"), None), P("img"), P(), P()),
        out_specs=(P("img"), P(("img", "txt"), None), P(("txt", "img"), None)),
        check_vma=False,
    )
```

time: 1210 us -> 69.3 us (0.06)
  the two profiles are of different devices: /device:TPU:192 before, /device:TPU:2 now
where the time goes in v1:
time: 69.3 us; the launch traced here: 69 us
  Pallas kernels  63.1 us (91%)
  local copies, waits for them, and re-layouts  4 us (6%)
  between operations  1.94 us (3%)
    pallas_call x1, Pallas kernels, per_device(): pl.pallas_call(kernel, out_shape=(jax.ShapeDtypeStruct((1, 128), F32), ja...  63.1 us
    unnamed x9, local copies, waits for them, and re-layouts  4 us

profile of v1, /device:TPU:2, one launch (start us, length us, event | category | flops | bytes accessed | tf_op | source)
XLA Modules:
  0.0 69.0 jit_solution(14713569133719756239)
XLA Ops:
  1.9 0.0 copy-start.2
  1.9 0.6 copy-done.2
  2.6 0.0 copy-start
  2.6 0.8 %copy-done = f32[16,768]{1,0:T(8,128)S(1)} copy-done((f32[16,768]{1,0:T(8,128)S(1)}, f32[16,768]{1,0:T(8,128)}, u32[]{:S(2)}) %copy-start) | copy-done | bytes 49176
  3.4 0.0 copy-start.1
  3.4 0.8 %copy-done.1 = f32[16,768]{1,0:T(8,128)S(1)} copy-done((f32[16,768]{1,0:T(8,128)S(1)}, f32[16,768]{1,0:T(8,128)}, u32[]{:S(2)}) %copy-start.1) | copy-done | bytes 49176
  4.2 63.1 %contrastive.1 = (f32[1,128]{1,0:T(1,128)S(1)}, f32[16,768]{1,0:T(8,128)S(1)}, f32[16,768]{1,0:T(8,128)S(1)}) custom-call(f32[1]{0:T(128)S(6)} %copy.11.log_scale_ref, f32[1]{0:T(128)S(6)} %copy.12.bias_ref, s32[1,128]{1,0:T(1,128)S(1)} %bitcast.2, f32[16,768]{1,0:T(8,128)S(1)} %copy-done, f32[16,768]{1,0:T(8,128)S(1)} %copy-done.1), custom_call_target="tpu_custom_call" | custom-call | tf_op jit(solution)/shard_map/contrastive/pallas_call | solution.py:348
  67.2 0.5 copy.13
  67.8 0.6 copy.14
  68.4 0.6 copy.15
Async XLA Ops:
  1.9 0.7 copy-start.2
  2.6 0.8 %copy-start = (f32[16,768]{1,0:T(8,128)S(1)}, f32[16,768]{1,0:T(8,128)}, u32[]{:S(2)}) copy-start(f32[16,768]{1,0:T(8,128)} %image_ref.1) | copy-start | bytes 147460
  3.4 0.8 %copy-start.1 = (f32[16,768]{1,0:T(8,128)S(1)}, f32[16,768]{1,0:T(8,128)}, u32[]{:S(2)}) copy-start(f32[16,768]{1,0:T(8,128)} %text_ref.1) | copy-start | bytes 147460

commit v2 on v1

v2 whole, which is shorter than its diff:
```python
import functools

import jax
import jax.numpy as jnp
from jax import lax
from jax.experimental import pallas as pl
from jax.experimental.pallas import tpu as pltpu
from jax.sharding import PartitionSpec as P

MESH = pl.DeviceIdType.MESH
NX, NY, NZ, ZLO = 4, 8, 12, 3
ROWS, WIDTH = 16, 768
CA = 256
CB = WIDTH - CA
TEXTS = 2 * NZ * ROWS
F32, BF16 = jnp.float32, jnp.bfloat16
COPIES = 128
STEP = (0, 1, -1)
RELAYS = (
    ((0, 1), (0, 2), 3),
    ((0, 1), (2, 2), 2),
    ((0, 3), (1, 2), -2),
    ((0, 1), (1, 1), 1),
    ((0, 1), (2, 1), -1),
    ((0, 3), (2, 3), -1),
    ((0, 3), (1, 3), 1),
)
BLOCK = NX * 4 * ROWS
NEAR, FAR = 0, 1


def at_y(by):
    return (by + 1) % NY


def halves(value):
    high = value.astype(BF16)
    return high, (value - high.astype(F32)).astype(BF16)


def dot3(ah, al, bh, bl, dims):
    def dot(a, b):
        return lax.dot_general(a, b, (dims, ((), ())), preferred_element_type=F32)

    return dot(ah, bh) + (dot(ah, bl) + dot(al, bh))


def kernel(
    log_scale_ref, bias_ref, pairs_ref, image_ref, text_ref,
    loss_ref, image_grad_ref, text_grad_ref,
    ga, gb, tx, xh, xl, th, tl, dh, dl, pc,
    xga, xgb, tg, rxb, rya, ryb, rxa, rc, rz, rk, py, px, ly, lx, lz,
    local_sem, send_sem, recv_sem,
):
    img, txt = lax.axis_index("img"), lax.axis_index("txt")
    column = lax.div(img, ZLO)
    x, y = lax.div(column, NY), lax.rem(column, NY)
    core = lax.rem(txt, 2)
    z = lax.div(txt, 2) * ZLO + lax.rem(img, ZLO)
    way = 1 - 2 * core

    def moved(at, by, size):
        return lax.rem(at + way * by + 2 * size, size)

    def device(at_x, at_y, at_z, at_core):
        return (
            (at_x * NY + at_y) * ZLO + lax.rem(at_z, ZLO),
            lax.div(at_z, ZLO) * 2 + at_core,
        )

    def along_x(by):
        return device(moved(x, by, NX), y, z, core)

    def along_y(by):
        return device(x, moved(y, by, NY), z, core)

    def along_z(by):
        return device(x, y, moved(z, by, NZ), core)

    sibling = device(x, y, z, 1 - core)
    peers = [along_z(by) for by in (3, -3, 2, -2)]
    peers += [along_y(by) for by in (2, -2)] + [along_x(2)]
    peers += [along(by) for along in (along_x, along_y, along_z) for by in (1, -1)]
    peers.append(sibling)

    copies = [
        pltpu.make_async_copy(image_ref.at[:, pl.ds(0, CA)], ga.at[at_y(0), 0], local_sem.at[0]),
        pltpu.make_async_copy(image_ref.at[:, pl.ds(CA, CB)], gb.at[0, at_y(0)], local_sem.at[1]),
        pltpu.make_async_copy(text_ref, tx.at[0, 0, 0], local_sem.at[2]),
    ]
    for copy in copies:
        copy.start()

    barrier = pltpu.get_barrier_semaphore()
    for peer in peers:
        pl.semaphore_signal(barrier, inc=1, device_id=peer, device_id_type=MESH)

    lane = lax.broadcasted_iota(jnp.int32, (8, 128), 1)
    row = lax.broadcasted_iota(jnp.int32, (8, 128), 0)
    own = 2 * (x * NY + y)
    pairs_row = jnp.broadcast_to(pairs_ref[...].astype(F32), (8, 128))
    tile = jnp.zeros((8, 128), F32)
    for half in range(2):
        picked = jnp.where(lane == txt * ROWS + half * 8 + row, pairs_row, 0.0)
        tile = jnp.where(lane == own + half, jnp.sum(picked, axis=1, keepdims=True), tile)
    py[1] = tile

    pl.semaphore_wait(barrier, len(peers))
    for copy in copies:
        copy.wait()

    started = []

    def send(source, target, to):
        at = len(started)
        copy = pltpu.make_async_remote_copy(
            src_ref=source,
            dst_ref=target,
            send_sem=send_sem.at[at],
            recv_sem=recv_sem.at[at],
            device_id=to,
            device_id_type=MESH,
        )
        copy.start()
        started.append(copy)
        return copy

    def arrived(*copies):
        for copy in copies:
            copy.wait_recv()

    def pass_on(slot):
        return [
            send(slot(at_y(2)), slot(at_y(4)), along_y(2)),
            send(slot(at_y(2)), slot(at_y(3)), along_y(1)),
            send(slot(at_y(-2)), slot(at_y(-3)), along_y(-1)),
        ]

    def b_along_x(low, count):
        return [
            send(gb.at[0, pl.ds(low, count)], gb.at[by % NX, pl.ds(low, count)], along_x(by))
            for by in (2, 1, -1)
        ]

    def b_along_y(*steps):
        return {by: send(gb.at[0, 1], gb.at[0, at_y(by)], along_y(by)) for by in steps}

    b_x = [None, None]
    b_y = b_along_y(2, -2)
    t_far = [send(tx.at[0, 0, 0], tx.at[0, 0, k], along_z(by)) for k, by in ((1, 3), (3, -3))]
    a_x = [send(ga.at[1, 0], ga.at[1, by % NX], along_x(by)) for by in (2, 1, -1)]
    b_y |= b_along_y(1, -1)
    b_x[NEAR] = b_along_x(1, 1)
    arrived(*a_x)
    arrived(b_y[2], b_y[-2])
    b_far = pass_on(lambda p: gb.at[0, p])
    b_x[NEAR] += b_along_x(3, 1)
    b_x[FAR] = b_along_x(7, 1)
    a_y = {by: send(ga.at[1], ga.at[at_y(by)], along_y(by)) for by in (2, -2)}
    p_y = {by: send(py.at[1], py.at[at_y(by)], along_y(by)) for by in (2, -2, 1, -1)}
    t_near = [send(tx.at[0, 0, 0], tx.at[0, e, 0], along_z(STEP[e])) for e in (1, 2)]
    arrived(b_y[1], b_y[-1])
    b_x[NEAR] += b_along_x(0, 1) + b_along_x(2, 1)
    arrived(*t_far)
    for near, far, by in RELAYS:
        t_near.append(send(tx.at[(0,) + near], tx.at[(0,) + far], along_z(by)))
    t_core = [send(tx.at[0, 0, pl.ds(0, 2)], tx.at[1, 0, pl.ds(0, 2)], sibling)]
    t_core.append(send(tx.at[0, 0, 3], tx.at[1, 0, 3], sibling))
    a_y |= {by: send(ga.at[1], ga.at[at_y(by)], along_y(by)) for by in (1, -1)}
    arrived(p_y[2], p_y[-2])
    p_far = pass_on(lambda p: py.at[p])
    arrived(*b_far)
    b_x[FAR] += b_along_x(4, 3)
    arrived(a_y[2], a_y[-2])
    a_far = pass_on(lambda p: ga.at[p])
    arrived(p_y[1], p_y[-1], *p_far)
    px[0] = jnp.sum(py[...], axis=0)
    p_x = [send(px.at[0], px.at[by % NX], along_x(by)) for by in (2, 1, -1)]

    places = lax.broadcasted_iota(jnp.int32, (8, TEXTS), 1)
    slot = lax.div(places, ROWS)
    ids = places
    for s in range(2):
        for e in range(3):
            for k in range(4):
                at = (s * 3 + e) * 4 + k
                by = 3 * k + STEP[e]
                at_z = moved(z, by if s else -by, NZ)
                at_core = 1 - core if s else core
                owner = lax.div(at_z, ZLO) * 2 + at_core
                base = owner * (NX * NY * ZLO * ROWS) + (column * ZLO + lax.rem(at_z, ZLO)) * ROWS
                ids = jnp.where(slot == at, places + (base - at * ROWS), ids)
    ids = ids.astype(F32)[0:1]

    arrived(*t_near)
    t_core.append(send(tx.at[0, 0, 2], tx.at[1, 0, 2], sibling))
    t_core.append(send(tx.at[0, pl.ds(1, 2)], tx.at[1, pl.ds(1, 2)], sibling))

    arrived(*p_x)
    matched = jnp.sum(px[...], axis=0)
    groups = [
        (block, ox, inner, half)
        for block in (NEAR, FAR)
        for ox in range(NX)
        for inner in range(4)
        for half in range(2)
    ]

    def lane_of(block, ox, inner, half):
        oy = block * 4 + inner - 1
        return 2 * (moved(x, -ox, NX) * NY + moved(y, -oy, NY)) + half

    for at, group in enumerate(groups):
        picked = jnp.where(lane == lane_of(*group), matched, 0.0)
        spread = jnp.broadcast_to(jnp.sum(picked, axis=1, keepdims=True), (8, 128))
        pc[pl.ds(at * 8, 8), :] = spread

    def split_texts(s):
        high, low = halves(tx[s].reshape(NZ * ROWS, WIDTH))
        th[pl.ds(s * NZ * ROWS, NZ * ROWS), :] = high
        tl[pl.ds(s * NZ * ROWS, NZ * ROWS), :] = low

    def split_images(block):
        for ox in range(NX):
            rows = pl.ds(block * BLOCK + ox * 4 * ROWS, 4 * ROWS)
            high, low = halves(ga[pl.ds(block * 4, 4), ox].reshape(4 * ROWS, CA))
            xh[rows, pl.ds(0, CA)] = high
            xl[rows, pl.ds(0, CA)] = low
            high, low = halves(gb[ox, pl.ds(block * 4, 4)].reshape(4 * ROWS, CB))
            xh[rows, pl.ds(CA, CB)] = high
            xl[rows, pl.ds(CA, CB)] = low

    scale = jnp.exp(jnp.full((8, 128), log_scale_ref[0], F32))[0:1, 0:1]
    shift = bias_ref[0]

    def slopes(block, losses):
        rows = pl.ds(block * BLOCK, BLOCK)
        dots = dot3(xh[rows, :], xl[rows, :], th[...], tl[...], ((1,), (1,)))
        logits = scale * dots + shift
        match = jnp.concatenate([pc[rows, :]] * (TEXTS // 128), axis=1) == ids
        signed = jnp.where(match, -logits, logits)
        small = jnp.exp(-jnp.abs(logits))
        loss = jnp.maximum(signed, 0.0) + jnp.log1p(small)
        loss = sum(loss[:, at * 128 : (at + 1) * 128] for at in range(TEXTS // 128))
        loss = jnp.sum(loss, axis=1, keepdims=True)
        for at, group in enumerate(groups[block * 32 : (block + 1) * 32]):
            losses = jnp.where(lane == lane_of(*group), loss[at * 8 : at * 8 + 8], losses)
        part = 1.0 / (1.0 + small)
        chance = jnp.where(signed >= 0.0, part, small * part)
        high, low = halves(scale * jnp.where(match, -chance, chance))
        dh[rows, :] = high
        dl[rows, :] = low
        return losses

    def image_terms(block):
        rows = pl.ds(block * BLOCK, BLOCK)
        grad = dot3(dh[rows, :], dl[rows, :], th[...], tl[...], ((1,), (0,)))
        inner = pl.ds(block * 4, 4)
        for ox in range(NX):
            part = grad[ox * 4 * ROWS : (ox + 1) * 4 * ROWS].reshape(4, ROWS, WIDTH)
            xgb[ox, inner] = part[:, :, CA:]
            xga[inner, ox] = part[:, :, :CA]

    def terms_along_x(block):
        inner = pl.ds(block * 4, 4)
        return [
            send(xgb.at[ox, inner], rxb.at[ox - 1, inner], along_x(-ox)) for ox in (2, 1, 3)
        ]

    def far_terms(source, target):
        return [
            send(source(at_y(4)), target(at_y(4)), along_y(-2)),
            send(source(at_y(3)), target(at_y(3)), along_y(-1)),
            send(source(at_y(-3)), target(at_y(-3)), along_y(1)),
        ]

    def text_terms(low, count):
        cols = pl.ds(low * ROWS, count * ROWS)
        part = dot3(dh[:, cols], dl[:, cols], xh[...], xl[...], ((0,), (0,)))
        part = part.reshape(count, ROWS, WIDTH)
        for i in range(count):
            s, rest = divmod(low + i, 12)
            e, k = divmod(rest, 4)
            tg[s, e, k] = part[i]

    split_texts(0)
    arrived(*t_core)
    split_texts(1)
    arrived(a_y[1], a_y[-1], *b_x[NEAR])
    split_images(NEAR)
    losses = slopes(NEAR, jnp.zeros((8, 128), F32))
    image_terms(NEAR)
    arrived(*a_far, *b_x[FAR])
    split_images(FAR)
    lx[0] = slopes(FAR, losses)
    l_x = [send(lx.at[0], lx.at[by % NX], along_x(by)) for by in (2, 1, -1)]
    image_terms(FAR)
    ra_far = far_terms(lambda p: xga.at[p], lambda p: rya.at[p])
    r_far = terms_along_x(FAR)

    text_terms(8, 16)
    r_core = send(tg.at[1], rc, sibling)
    r_near = terms_along_x(NEAR)
    arrived(*l_x)
    ly[1] = jnp.sum(lx[...], axis=0)
    l_y = {by: send(ly.at[1], ly.at[at_y(by)], along_y(by)) for by in (2, -2, 1, -1)}
    ra_near = [send(xga.at[at_y(by)], rya.at[at_y(by)], along_y(-by)) for by in (1, -1)]
    text_terms(0, 8)
    arrived(r_core)
    tg[0] += rc[...]
    r_z = {}
    for near, far, by in RELAYS:
        r_z.setdefault(near, []).append(send(tg.at[(0,) + far], rz.at[far], along_z(-by)))
    r_last = [send(tg.at[0, e, 0], rz.at[e, 0], along_z(-STEP[e])) for e in (1, 2)]

    arrived(l_y[2], l_y[-2])
    l_far = pass_on(lambda p: ly.at[p])
    arrived(*ra_far)
    xga[3] += rya[4] + rya[5]
    xga[7] += rya[6]
    ra_near += [send(xga.at[3], rya.at[3], along_y(-2)), send(xga.at[7], rya.at[7], along_y(2))]

    arrived(*r_far)
    xgb[0, pl.ds(4, 4)] += rxb[0, pl.ds(4, 4)] + rxb[1, pl.ds(4, 4)] + rxb[2, pl.ds(4, 4)]
    rb_far = far_terms(lambda p: xgb.at[0, p], lambda p: ryb.at[p])

    arrived(l_y[1], l_y[-1], *l_far)
    lz[0, 0] = jnp.sum(ly[...], axis=0)
    l_core = send(lz.at[0, 0], lz.at[0, 1], sibling)
    arrived(l_core)
    l_z = [send(lz.at[0], lz.at[k], along_z(by)) for k, by in ((1, 3), (3, -3))]

    for at, (near, by) in enumerate((((0, 1), 3), ((0, 3), -3))):
        arrived(*r_z[near])
        tg[(0,) + near] += sum(rz[far] for relay, far, _ in RELAYS if relay == near)
        r_last.append(send(tg.at[(0,) + near], rk.at[at], along_z(-by)))

    arrived(*r_near)
    xgb[0, pl.ds(0, 4)] += rxb[0, pl.ds(0, 4)] + rxb[1, pl.ds(0, 4)] + rxb[2, pl.ds(0, 4)]
    arrived(*rb_far)
    xgb[0, 3] += ryb[4] + ryb[5]
    xgb[0, 7] += ryb[6]
    rb = [send(xgb.at[0, at_y(by)], ryb.at[at_y(by)], along_y(-by)) for by in (2, -2, 1, -1)]

    arrived(*l_z)
    l_last = send(lz.at[1], lz.at[2], along_z(3))

    arrived(*ra_near)
    xga[1] += (rya[0] + rya[2]) + (rya[3] + rya[7])
    r_a = [send(xga.at[1, ox], rxa.at[ox - 1], along_x(-ox)) for ox in (2, 1, 3)]

    arrived(*r_a)
    image_grad_ref[:, pl.ds(0, CA)] = xga[1, 0] + rxa[0] + rxa[1] + rxa[2]
    arrived(*r_last)
    text_grad_ref[...] = (tg[0, 0, 0] + rz[1, 0] + rz[2, 0]) + (rk[0] + rk[1])
    arrived(*rb)
    total = xgb[0, 1]
    for by in (1, -1, 2, -2):
        total += ryb[at_y(by)]
    image_grad_ref[:, pl.ds(CA, CB)] = total

    arrived(l_last)
    out = jnp.zeros((8, 128), F32)
    for k in range(4):
        for s in range(2):
            at_txt = lax.div(moved(z, -3 * k, NZ), ZLO) * 2 + (1 - core if s else core)
            for half in range(2):
                picked = jnp.where(lane == own + half, lz[k, s], 0.0)
                value = jnp.sum(picked, axis=1, keepdims=True)
                out = jnp.where(lane == at_txt * ROWS + half * 8 + row, value, out)
    loss_ref[...] = jnp.sum(out, axis=0, keepdims=True)

    for copy in started:
        copy.wait_send()


def per_device(image_emb, text_emb, pairs, log_scale, bias):
    vmem = pl.BlockSpec(memory_space=pltpu.VMEM)
    smem = pl.BlockSpec(memory_space=pltpu.SMEM)
    hbm = pl.BlockSpec(memory_space=pl.ANY)
    images = NX * NY * ROWS
    in_hbm = functools.partial(pltpu.with_memory_space_constraint, memory_space=pltpu.HBM)
    loss, image_grad, text_grad = pl.pallas_call(
        kernel,
        out_shape=(
            jax.ShapeDtypeStruct((1, 128), F32),
            jax.ShapeDtypeStruct((ROWS, WIDTH), F32),
            jax.ShapeDtypeStruct((ROWS, WIDTH), F32),
        ),
        in_specs=[smem, smem, vmem, hbm, hbm],
        out_specs=(vmem, vmem, vmem),
        scratch_shapes=[
            pltpu.VMEM((NY, NX, ROWS, CA), F32),
            pltpu.VMEM((NX, NY, ROWS, CB), F32),
            pltpu.VMEM((2, 3, 4, ROWS, WIDTH), F32),
            pltpu.VMEM((images, WIDTH), BF16),
            pltpu.VMEM((images, WIDTH), BF16),
            pltpu.VMEM((TEXTS, WIDTH), BF16),
            pltpu.VMEM((TEXTS, WIDTH), BF16),
            pltpu.VMEM((images, TEXTS), BF16),
            pltpu.VMEM((images, TEXTS), BF16),
            pltpu.VMEM((images, 128), F32),
            pltpu.VMEM((NY, NX, ROWS, CA), F32),
            pltpu.VMEM((NX, NY, ROWS, CB), F32),
            pltpu.VMEM((2, 3, 4, ROWS, WIDTH), F32),
            pltpu.VMEM((3, NY, ROWS, CB), F32),
            pltpu.VMEM((NY, NX, ROWS, CA), F32),
            pltpu.VMEM((NY, ROWS, CB), F32),
            pltpu.VMEM((3, ROWS, CA), F32),
            pltpu.VMEM((3, 4, ROWS, WIDTH), F32),
            pltpu.VMEM((3, 4, ROWS, WIDTH), F32),
            pltpu.VMEM((2, ROWS, WIDTH), F32),
            pltpu.VMEM((NY, 8, 128), F32),
            pltpu.VMEM((NX, 8, 128), F32),
            pltpu.VMEM((NY, 8, 128), F32),
            pltpu.VMEM((NX, 8, 128), F32),
            pltpu.VMEM((4, 2, 8, 128), F32),
            pltpu.SemaphoreType.DMA((3,)),
            pltpu.SemaphoreType.DMA((COPIES,)),
            pltpu.SemaphoreType.DMA((COPIES,)),
        ],
        compiler_params=pltpu.CompilerParams(
            collective_id=0, has_side_effects=True, vmem_limit_bytes=40 * 2**20
        ),
        name="contrastive",
    )(log_scale, bias, *(in_hbm(part) for part in (pairs.reshape(1, 128), image_emb, text_emb)))
    return loss.reshape(128), image_grad, text_grad


def solution(mesh):
    return jax.shard_map(
        per_device,
        mesh=mesh,
        in_specs=(P(("img", "txt"), None), P(("txt", "img"), None), P("img"), P(), P()),
        out_specs=(P("img"), P(("img", "txt"), None), P(("txt", "img"), None)),
        check_vma=False,
    )
```

time: 69.3 us -> 65.7 us (0.948)
  the two profiles are of different devices: /device:TPU:2 before, /device:TPU:1 now
where the time goes in v2:
time: 65.7 us; the launch traced here: 65.6 us
  Pallas kernels  61.9 us (94%)
  between operations  1.93 us (3%)
  local copies, waits for them, and re-layouts  1.75 us (3%)
    pallas_call x1, Pallas kernels, per_device(): pl.pallas_call(kernel, out_shape=(jax.ShapeDtypeStruct((1, 128), F32), ja...  61.9 us
    unnamed x3, local copies, waits for them, and re-layouts  1.75 us

profile of v2, /device:TPU:1, one launch (start us, length us, event | category | flops | bytes accessed | tf_op | source)
XLA Modules:
  0.0 65.6 jit_solution(12109335055343786921)
XLA Ops:
  1.9 61.9 %contrastive.1 = (f32[1,128]{1,0:T(1,128)S(1)}, f32[16,768]{1,0:T(8,128)S(1)}, f32[16,768]{1,0:T(8,128)S(1)}) custom-call(f32[1]{0:T(128)S(6)} %copy.11.log_scale_ref, f32[1]{0:T(128)S(6)} %copy.12.bias_ref, s32[1,128]{1,0:T(1,128)} %bitcast.3, f32[16,768]{1,0:T(8,128)} %image_ref.1, f32[16,768]{1,0:T(8,128)} %text_ref.1), custom_call_target="tpu_custom_call" | custom-call | tf_op jit(solution)/shard_map/contrastive/pallas_call | solution.py:383
  63.8 0.5 copy.13
  64.3 0.6 copy.14
  65.0 0.6 copy.15

commit v3 on v2

--- a/solution.py
+++ b/solution.py
@@ -50,7 +50,7 @@
     loss_ref, image_grad_ref, text_grad_ref,
     ga, gb, tx, xh, xl, th, tl, dh, dl, pc,
     xga, xgb, tg, rxb, rya, ryb, rxa, rc, rz, rk, py, px, ly, lx, lz,
-    local_sem, send_sem, recv_sem,
+    pairs_here, local_sem, send_sem, recv_sem,
 ):
     img, txt = lax.axis_index("img"), lax.axis_index("txt")
     column = lax.div(img, ZLO)
@@ -83,7 +83,12 @@
     peers += [along(by) for along in (along_x, along_y, along_z) for by in (1, -1)]
     peers.append(sibling)
 
+    barrier = pltpu.get_barrier_semaphore()
+    for peer in peers:
+        pl.semaphore_signal(barrier, inc=1, device_id=peer, device_id_type=MESH)
+
     copies = [
+        pltpu.make_async_copy(pairs_ref, pairs_here, local_sem.at[3]),
         pltpu.make_async_copy(image_ref.at[:, pl.ds(0, CA)], ga.at[at_y(0), 0], local_sem.at[0]),
         pltpu.make_async_copy(image_ref.at[:, pl.ds(CA, CB)], gb.at[0, at_y(0)], local_sem.at[1]),
         pltpu.make_async_copy(text_ref, tx.at[0, 0, 0], local_sem.at[2]),
@@ -91,14 +96,11 @@
     for copy in copies:
         copy.start()
 
-    barrier = pltpu.get_barrier_semaphore()
-    for peer in peers:
-        pl.semaphore_signal(barrier, inc=1, device_id=peer, device_id_type=MESH)
-
     lane = lax.broadcasted_iota(jnp.int32, (8, 128), 1)
     row = lax.broadcasted_iota(jnp.int32, (8, 128), 0)
     own = 2 * (x * NY + y)
-    pairs_row = jnp.broadcast_to(pairs_ref[...].astype(F32), (8, 128))
+    copies[0].wait()
+    pairs_row = jnp.broadcast_to(pairs_here[...].astype(F32), (8, 128))
     tile = jnp.zeros((8, 128), F32)
     for half in range(2):
         picked = jnp.where(lane == txt * ROWS + half * 8 + row, pairs_row, 0.0)
@@ -106,8 +108,6 @@
     py[1] = tile
 
     pl.semaphore_wait(barrier, len(peers))
-    for copy in copies:
-        copy.wait()
 
     started = []
 
@@ -136,6 +136,8 @@
             send(slot(at_y(-2)), slot(at_y(-3)), along_y(-1)),
         ]
 
+    own_a, own_b = image_ref.at[:, pl.ds(0, CA)], image_ref.at[:, pl.ds(CA, CB)]
+
     def b_along_x(low, count):
         return [
             send(gb.at[0, pl.ds(low, count)], gb.at[by % NX, pl.ds(low, count)], along_x(by))
@@ -143,27 +145,29 @@
         ]
 
     def b_along_y(*steps):
-        return {by: send(gb.at[0, 1], gb.at[0, at_y(by)], along_y(by)) for by in steps}
+        return {by: send(own_b, gb.at[0, at_y(by)], along_y(by)) for by in steps}
 
     b_x = [None, None]
     b_y = b_along_y(2, -2)
-    t_far = [send(tx.at[0, 0, 0], tx.at[0, 0, k], along_z(by)) for k, by in ((1, 3), (3, -3))]
-    a_x = [send(ga.at[1, 0], ga.at[1, by % NX], along_x(by)) for by in (2, 1, -1)]
+    t_far = [send(text_ref, tx.at[0, 0, k], along_z(by)) for k, by in ((1, 3), (3, -3))]
+    a_x = [send(own_a, ga.at[1, by % NX], along_x(by)) for by in (2, 1, -1)]
+    t_near = {(e, 0): send(text_ref, tx.at[0, e, 0], along_z(STEP[e])) for e in (1, 2)}
     b_y |= b_along_y(1, -1)
+    for copy in copies[1:]:
+        copy.wait()
     b_x[NEAR] = b_along_x(1, 1)
     arrived(*a_x)
+    a_y = {by: send(ga.at[1], ga.at[at_y(by)], along_y(by)) for by in (2, -2)}
     arrived(b_y[2], b_y[-2])
     b_far = pass_on(lambda p: gb.at[0, p])
     b_x[NEAR] += b_along_x(3, 1)
     b_x[FAR] = b_along_x(7, 1)
-    a_y = {by: send(ga.at[1], ga.at[at_y(by)], along_y(by)) for by in (2, -2)}
     p_y = {by: send(py.at[1], py.at[at_y(by)], along_y(by)) for by in (2, -2, 1, -1)}
-    t_near = [send(tx.at[0, 0, 0], tx.at[0, e, 0], along_z(STEP[e])) for e in (1, 2)]
     arrived(b_y[1], b_y[-1])
     b_x[NEAR] += b_along_x(0, 1) + b_along_x(2, 1)
     arrived(*t_far)
     for near, far, by in RELAYS:
-        t_near.append(send(tx.at[(0,) + near], tx.at[(0,) + far], along_z(by)))
+        t_near[far] = send(tx.at[(0,) + near], tx.at[(0,) + far], along_z(by))
     t_core = [send(tx.at[0, 0, pl.ds(0, 2)], tx.at[1, 0, pl.ds(0, 2)], sibling)]
     t_core.append(send(tx.at[0, 0, 3], tx.at[1, 0, 3], sibling))
     a_y |= {by: send(ga.at[1], ga.at[at_y(by)], along_y(by)) for by in (1, -1)}
@@ -192,9 +196,9 @@
                 ids = jnp.where(slot == at, places + (base - at * ROWS), ids)
     ids = ids.astype(F32)[0:1]
 
-    arrived(*t_near)
-    t_core.append(send(tx.at[0, 0, 2], tx.at[1, 0, 2], sibling))
-    t_core.append(send(tx.at[0, pl.ds(1, 2)], tx.at[1, pl.ds(1, 2)], sibling))
+    for far in ((1, 0), (2, 0), (1, 1), (2, 1), (2, 3), (1, 3), (2, 2), (1, 2), (0, 2)):
+        arrived(t_near[far])
+        t_core.append(send(tx.at[(0,) + far], tx.at[(1,) + far], sibling))
 
     arrived(*p_x)
     matched = jnp.sum(px[...], axis=0)
@@ -387,7 +391,7 @@
             jax.ShapeDtypeStruct((ROWS, WIDTH), F32),
             jax.ShapeDtypeStruct((ROWS, WIDTH), F32),
         ),
-        in_specs=[smem, smem, vmem, hbm, hbm],
+        in_specs=[smem, smem, hbm, hbm, hbm],
         out_specs=(vmem, vmem, vmem),
         scratch_shapes=[
             pltpu.VMEM((NY, NX, ROWS, CA), F32),
@@ -415,7 +419,8 @@
             pltpu.VMEM((NY, 8, 128), F32),
             pltpu.VMEM((NX, 8, 128), F32),
             pltpu.VMEM((4, 2, 8, 128), F32),
-            pltpu.SemaphoreType.DMA((3,)),
+            pltpu.VMEM((1, 128), jnp.int32),
+            pltpu.SemaphoreType.DMA((4,)),
             pltpu.SemaphoreType.DMA((COPIES,)),
             pltpu.SemaphoreType.DMA((COPIES,)),
         ],

time: 65.7 us -> 64.9 us (0.988)
  Pallas kernels: 61.9 us -> 61 us
    pallas_call x1, Pallas kernels: 61.9 us -> 61 us  [per_device(): pl.pallas_call(kernel, out_shape=(jax.ShapeDtypeStruct((1, 128), F32), ja...]
where the time goes in v3:
time: 64.9 us; the launch traced here: 64.7 us
  Pallas kernels  61 us (94%)
  between operations  1.93 us (3%)
  local copies, waits for them, and re-layouts  1.75 us (3%)
    pallas_call x1, Pallas kernels, per_device(): pl.pallas_call(kernel, out_shape=(jax.ShapeDtypeStruct((1, 128), F32), ja...  61 us
    unnamed x3, local copies, waits for them, and re-layouts  1.75 us

profile of v3, /device:TPU:1, one launch (start us, length us, event | category | flops | bytes accessed | tf_op | source)
XLA Modules:
  0.0 64.7 jit_solution(9430459284169229662)
XLA Ops:
  1.9 61.0 %contrastive.1 = (f32[1,128]{1,0:T(1,128)S(1)}, f32[16,768]{1,0:T(8,128)S(1)}, f32[16,768]{1,0:T(8,128)S(1)}) custom-call(f32[1]{0:T(128)S(6)} %copy.11.log_scale_ref, f32[1]{0:T(128)S(6)} %copy.12.bias_ref, s32[1,128]{1,0:T(1,128)} %bitcast.3, f32[16,768]{1,0:T(8,128)} %image_ref.1, f32[16,768]{1,0:T(8,128)} %text_ref.1), custom_call_target="tpu_custom_call" | custom-call | tf_op jit(solution)/shard_map/contrastive/pallas_call | solution.py:387
  62.9 0.5 copy.13
  63.4 0.6 copy.14
  64.1 0.6 copy.15

commit v4 on v3

--- a/solution.py
+++ b/solution.py
@@ -303,18 +303,20 @@
     r_far = terms_along_x(FAR)
 
     text_terms(8, 16)
-    r_core = send(tg.at[1], rc, sibling)
+    r_core = {e: send(tg.at[1, e], rc.at[e], sibling) for e in (0, 2, 1)}
     r_near = terms_along_x(NEAR)
     arrived(*l_x)
     ly[1] = jnp.sum(lx[...], axis=0)
     l_y = {by: send(ly.at[1], ly.at[at_y(by)], along_y(by)) for by in (2, -2, 1, -1)}
     ra_near = [send(xga.at[at_y(by)], rya.at[at_y(by)], along_y(-by)) for by in (1, -1)]
     text_terms(0, 8)
-    arrived(r_core)
-    tg[0] += rc[...]
     r_z = {}
-    for near, far, by in RELAYS:
-        r_z.setdefault(near, []).append(send(tg.at[(0,) + far], rz.at[far], along_z(-by)))
+    for e in (0, 2, 1):
+        arrived(r_core[e])
+        tg[0, e] += rc[e]
+        for near, far, by in RELAYS:
+            if far[0] == e:
+                r_z.setdefault(near, []).append(send(tg.at[(0,) + far], rz.at[far], along_z(-by)))
     r_last = [send(tg.at[0, e, 0], rz.at[e, 0], along_z(-STEP[e])) for e in (1, 2)]
 
     arrived(l_y[2], l_y[-2])

time: 64.9 us -> 65.4 us (level)
  no operation moved by 1% of the time
where the time goes in v4:
time: 65.4 us; the launch traced here: 64.8 us
  Pallas kernels  61.1 us (93%)
  between operations  1.93 us (3%)
  local copies, waits for them, and re-layouts  1.75 us (3%)
    pallas_call x1, Pallas kernels, per_device(): pl.pallas_call(kernel, out_shape=(jax.ShapeDtypeStruct((1, 128), F32), ja...  61.1 us
    unnamed x3, local copies, waits for them, and re-layouts  1.75 us

profile of v4, /device:TPU:1, one launch (start us, length us, event | category | flops | bytes accessed | tf_op | source)
XLA Modules:
  0.0 64.8 jit_solution(14957477433248217196)
XLA Ops:
  1.9 61.1 %contrastive.1 = (f32[1,128]{1,0:T(1,128)S(1)}, f32[16,768]{1,0:T(8,128)S(1)}, f32[16,768]{1,0:T(8,128)S(1)}) custom-call(f32[1]{0:T(128)S(6)} %copy.11.log_scale_ref, f32[1]{0:T(128)S(6)} %copy.12.bias_ref, s32[1,128]{1,0:T(1,128)} %bitcast.3, f32[16,768]{1,0:T(8,128)} %image_ref.1, f32[16,768]{1,0:T(8,128)} %text_ref.1), custom_call_target="tpu_custom_call" | custom-call | tf_op jit(solution)/shard_map/contrastive/pallas_call | solution.py:389
  63.0 0.5 copy.13
  63.5 0.6 copy.14
  64.1 0.6 copy.15
